TPU v7x, 32 devices: a whole 2x2x4 slice. The times are simulated.
32 devices in a mesh: tile: 8 (over z, y), lev: 4 (over x, core).
Axes of the slice: x: 2, y: 2, z: 4, core: 2. Of those that a mesh axis runs over, the one named last changes fastest.
Arguments:
- state: bfloat16 [4, 64, 512, 64], P(None, 'lev', 'tile'), may hold values from -6 to 6
- state_cotangent: bfloat16 [4, 64, 512, 64], P(None, 'lev', 'tile'), may hold values from -6 to 6
- diffusion: float32 [512, 64], P('tile'), may hold values from 0.05 to 0.24
- remap_weight: float32 [64, 4], replicated, may hold values from 0.05 to 0.5
- remap_band: int32 [64], replicated, may hold values from 0 to 60, as said below
- edge_table: int32 [8, 4, 4], P('tile'), may hold values from 0 to 7, as said below
- w_in: bfloat16 [1024, 256], replicated, may hold values from -0.375 to 0.375
- w_out: bfloat16 [256, 1024], replicated, may hold values from -0.1875 to 0.1875
Outputs:
- state_out: bfloat16 [4, 64, 512, 64], P(None, 'lev', 'tile')
- grad_state: bfloat16 [4, 64, 512, 64], P(None, 'lev', 'tile')
- grad_w_in: float32 [1024, 256], replicated
- grad_w_out: float32 [256, 1024], replicated
Inputs may be any that keep to these rules, and one draw needn't show every extreme that they name: `edge_table`: entry [t, e] describes edge e of tile t (0 first row, 1 last row, 2 first column, 3 last column): [t, e, 0] is the tile across it, [t, e, 1] that tile's matching edge, [t, e, 2] is 1 where the strip runs reversed and 0 else, [t, e, 3] the quarter turns 0 to 3 of the vector components. The matching is symmetric: the partner's entry points back, with the same reversal and the opposite turns modulo 4. The four edges of a tile meet four different tiles, none of them the tile itself. remap_band[k] lies between k - 2 and k + 1, clipped to the range; remap_band[0] is 0.
All inputs are finite; a program needn't handle non-finite values.
Results may differ from a plain program's by a relative error of at most 0.0075.
Values may be sent and summed in bfloat16 or wider, within the bound.
A program may use at most 128 MiB of HBM per device.

v0:
```python
import math
import jax
import jax.numpy as jnp
from jax import lax
from jax.sharding import PartitionSpec as P


def local_strips(block):
    return jnp.stack(
        [block[:, :, 0, :], block[:, :, -1, :], block[:, :, :, 0], block[:, :, :, -1]], axis=0
    )


def orient(strip, flipped, quarter):
    strip = jnp.where(flipped == 1, strip[..., ::-1], strip)
    cosine = (quarter == 0).astype(jnp.float32) - (quarter == 2).astype(jnp.float32)
    sine_part = (quarter == 1).astype(jnp.float32) - (quarter == 3).astype(jnp.float32)
    first = strip[0].astype(jnp.float32)
    second = strip[1].astype(jnp.float32)
    turned = jnp.stack(
        [cosine * first - sine_part * second, sine_part * first + cosine * second]
    ).astype(strip.dtype)
    return jnp.concatenate([turned, strip[2:]], axis=0)


def fetch_halo(block, table):
    strips = local_strips(block)
    targets = table[:, 0]
    sources = table[:, 1]
    piece = lax.all_gather(strips[None], "tile", axis=0, tiled=True)
    ranks = jnp.arange(piece.shape[0], dtype=jnp.int32)
    edge_ids = jnp.arange(4, dtype=jnp.int32)
    which = (
        (ranks[None, :, None] == targets[:, None, None])
        & (edge_ids[None, None, :] == sources[:, None, None])
    ).astype(jnp.bfloat16)
    picked = jnp.einsum("eqk,qkflc->eflc", which, piece, preferred_element_type=jnp.float32).astype(
        jnp.bfloat16
    )
    return jnp.stack([orient(picked[edge], table[edge, 2], table[edge, 3]) for edge in range(4)])


def neighbour_sum(block, halos):
    upper = jnp.concatenate([halos[0][:, :, None, :], block[:, :, :-1, :]], axis=2)
    lower = jnp.concatenate([block[:, :, 1:, :], halos[1][:, :, None, :]], axis=2)
    before = jnp.concatenate([halos[2][:, :, :, None], block[:, :, :, :-1]], axis=3)
    after = jnp.concatenate([block[:, :, :, 1:], halos[3][:, :, :, None]], axis=3)
    return upper + lower + before + after


def remap_matrix(weight, band):
    level_ids = jnp.arange(weight.shape[0], dtype=jnp.int32)
    matrix = jnp.zeros((weight.shape[0], weight.shape[0]), weight.dtype)
    for offset in range(weight.shape[1]):
        hits = (level_ids[None, :] == (band + offset)[:, None]).astype(weight.dtype)
        matrix = matrix + weight[:, offset][:, None] * hits
    return matrix


def band_remap(columns, weight, band):
    total = jnp.zeros(columns.shape, weight.dtype)
    for offset in range(weight.shape[1]):
        picked = jnp.take(columns, band + offset, axis=1).astype(weight.dtype)
        total = total + weight[:, offset][None, :, None] * picked
    return total.astype(jnp.bfloat16)


def contract(left, right, left_dim, right_dim):
    return lax.dot_general(
        left, right, (((left_dim,), (right_dim,)), ((), ())), preferred_element_type=jnp.float32
    )


def shards(state, state_cotangent, diffusion, remap_weight, remap_band, edge_table, w_in, w_out):
    tiles = lax.axis_size("tile")
    local_levels = state.shape[1]
    side = state.shape[3]
    levels = remap_weight.shape[0]
    features = w_in.shape[1]
    table = edge_table[0]
    values = state.astype(jnp.float32)
    halo = fetch_halo(state, table).astype(jnp.float32)
    moved = (values + diffusion * (neighbour_sum(values, halo) - 4.0 * values)).astype(jnp.bfloat16)
    flat_moved = moved.reshape(4, local_levels, side * side)
    flat_cotangent = state_cotangent.reshape(4, local_levels, side * side)
    whole = lax.all_to_all(flat_moved, "lev", split_axis=2, concat_axis=1, tiled=True)
    count = whole.shape[2]
    width = min(512, count)
    blocks = count // width
    remapped = band_remap(whole, remap_weight, remap_band)
    flat = remapped.reshape(features, count)

    def forward_block(index, output):
        cols = lax.dynamic_slice_in_dim(flat, index * width, width, 1)
        pre = jnp.dot(w_in, cols, preferred_element_type=jnp.float32)
        hidden = (pre * jax.nn.sigmoid(pre)).astype(jnp.bfloat16)
        result = (
            cols.astype(jnp.float32) + jnp.dot(w_out, hidden, preferred_element_type=jnp.float32)
        ).astype(jnp.bfloat16)
        return lax.dynamic_update_slice_in_dim(output, result, index * width, 1)

    output = lax.fori_loop(0, blocks, forward_block, jnp.zeros_like(flat))
    output = output.reshape(4, levels, count)
    state_back = lax.all_to_all(output, "lev", split_axis=1, concat_axis=2, tiled=True)
    grad_whole = lax.all_to_all(flat_cotangent, "lev", split_axis=2, concat_axis=1, tiled=True)
    grad_flat = grad_whole.reshape(features, count)

    def backward_block(index, carry):
        grad_in, grad_out, dflat = carry
        cols = lax.dynamic_slice_in_dim(flat, index * width, width, 1)
        grads = lax.dynamic_slice_in_dim(grad_flat, index * width, width, 1)
        pre = jnp.dot(w_in, cols, preferred_element_type=jnp.float32)
        sigma = jax.nn.sigmoid(pre)
        hidden = (pre * sigma).astype(jnp.bfloat16)
        back = contract(w_out, grads, 0, 0)
        slope = (sigma * (1.0 + pre * (1.0 - sigma)) * back).astype(jnp.bfloat16)
        grad_out = grad_out + contract(grads, hidden, 1, 1)
        grad_in = grad_in + contract(slope, cols, 1, 1)
        dcols = grads.astype(jnp.float32) + contract(w_in, slope, 0, 0)
        return (grad_in, grad_out, lax.dynamic_update_slice_in_dim(dflat, dcols, index * width, 1))

    start = (
        jnp.zeros(w_in.shape, jnp.float32),
        jnp.zeros(w_out.shape, jnp.float32),
        jnp.zeros((features, count), jnp.float32),
    )
    grad_in, grad_out, dflat = lax.fori_loop(0, blocks, backward_block, start)
    matrix = remap_matrix(remap_weight, remap_band)
    dmoved_cols = jnp.einsum(
        "kj,fkn->fjn", matrix, dflat.reshape(4, levels, count), precision=lax.Precision.HIGHEST
    ).astype(jnp.bfloat16)
    dmoved = lax.all_to_all(dmoved_cols, "lev", split_axis=1, concat_axis=2, tiled=True)
    grad_in, grad_out = lax.psum((grad_in, grad_out), ("tile", "lev"))
    dmoved = dmoved.reshape(4, local_levels, side, side)
    flux = (diffusion * dmoved.astype(jnp.float32)).astype(jnp.bfloat16)
    flux_halo = fetch_halo(flux, table).astype(jnp.float32)
    wide_flux = flux.astype(jnp.float32)
    grad_state = (
        dmoved.astype(jnp.float32) - 4.0 * wide_flux + neighbour_sum(wide_flux, flux_halo)
    ).astype(jnp.bfloat16)
    scale = 1.0 / math.sqrt(tiles * side * side)
    state_out = state_back.reshape(4, local_levels, side, side)
    return (state_out, grad_state, grad_in * scale, grad_out * scale)


def solution(mesh):
    placed = (
        P(None, "lev", "tile", None),
        P(None, "lev", "tile", None),
        P("tile", None),
        P(),
        P(),
        P("tile", None, None),
        P(),
        P(),
    )
    return jax.shard_map(
        shards,
        mesh=mesh,
        in_specs=placed,
        out_specs=(P(None, "lev", "tile", None), P(None, "lev", "tile", None), P(), P()),
        check_vma=False,
    )
```

profile of v0, /device:TPU:0, one launch (start us, length us, event | category | flops | bytes accessed | tf_op | source)
XLA Modules:
  0.0 324.4 jit_solution(15446711326868766442)
XLA Ops:
  8.2 2.1 fusion.102
  21.7 2.6 fusion.99
  24.3 2.7 fusion.100
  28.0 33.0 %all-gather = bf16[32,4,16,64]{3,2,1,0:T(8,128)(2,1)S(1)} all-gather(bf16[4,4,16,64]{3,2,1,0:T(8,128)(2,1)S(1)} %pad_maximum_fusion), channel_id=2, replica_groups=mesh['tile'=8,'lev'=4] {'tile'}, dimensions={0}, use_global_device_ids=true | all-gather | bytes 294912 | tf_op jit(solution)/shard_map/all_gather | solution.py:30
  67.6 5.7 %fusion.28 = bf16[4,16,64,64]{3,2,1,0:T(8,128)(2,1)} fusion(f32[4,16,63,64]{3,2,1,0:T(8,128)} %get-tuple-element.457, f32[4,16,1,64]{3,2,1,0:T(1,128)S(1)} %bitcast.284, f32[4,16,1,64]{3,2,1,0:T(1,128)S(1)} %bitcast.283, f32[4,16,63,64]{3,2,1,0:T(8,128)} %get-tuple-element.456, f32[4,16,64,63]{3,2,1,0:T(8,128)} %get-tuple-element.455, ...), kind=kLoop, calls=%fused_computation.46 | loop fusion | flops 3407872 | bytes 5259264 | tf_op jit(solution)/shard_map/convert_element_type | solution.py:83
  73.3 7.3 %copy.332 = bf16[4,16,64,64]{1,0,3,2:T(4,128)(2,1)} copy(bf16[4,16,64,64]{3,2,1,0:T(8,128)(2,1)} %fusion.28) | data formatting | bytes 1048576 | tf_op jit(solution)/shard_map/reshape | solution.py:84
  80.7 6.5 %reshape.228 = bf16[4,2,32768]{2,1,0:T(2,128)(2,1)} reshape(bf16[4096,4,16]{2,1,0:T(4,128)(2,1)} %bitcast.268) | data formatting | bytes 1048576
  87.2 3.5 %all-to-all-start = ((bf16[4,2,32768]{2,1,0:T(2,128)(2,1)}), bf16[4,2,32768]{2,1,0:T(2,128)(2,1)S(1)}, u32[]{:S(2)}, u32[]{:S(2)}) async-start(bf16[4,2,32768]{2,1,0:T(2,128)(2,1)} %reshape.228), calls=%async_computation | async-start | bytes 1048576 | tf_op jit(solution)/shard_map/all_to_all | solution.py:86
  90.7 4.9 %copy.317 = bf16[4,16,64,64]{1,0,3,2:T(4,128)(2,1)} copy(bf16[4,16,64,64]{3,2,1,0:T(8,128)(2,1)S(1)} %copy-done.10) | data formatting | bytes 1048576 | tf_op args[1]
  95.7 6.5 %reshape.230 = bf16[4,2,32768]{2,1,0:T(2,128)(2,1)} reshape(bf16[4096,4,16]{2,1,0:T(4,128)(2,1)} %bitcast.269) | data formatting | bytes 1048576
  102.1 3.7 %all-to-all-start.2 = ((bf16[4,2,32768]{2,1,0:T(2,128)(2,1)}), bf16[4,2,32768]{2,1,0:T(2,128)(2,1)S(1)}, u32[]{:S(2)}, u32[]{:S(2)}) async-start(bf16[4,2,32768]{2,1,0:T(2,128)(2,1)} %reshape.230), calls=%async_computation.2 | async-start | bytes 1048576 | tf_op jit(solution)/shard_map/all_to_all | solution.py:105
  105.9 4.1 %reshape.229 = bf16[4096,4,16]{2,1,0:T(4,128)(2,1)} reshape(bf16[4,2,32768]{2,1,0:T(2,128)(2,1)S(1)} %all-to-all-done) | data formatting | bytes 1048576
  110.0 5.5 %copy.303 = bf16[4,4,16,1024]{3,2,1,0:T(8,128)(2,1)S(1)} copy(bf16[4,4,16,1024]{2,0,3,1:T(4,128)(2,1)} %bitcast.270) | data formatting | bytes 1048576 | tf_op jit(solution)/shard_map/all_to_all | solution.py:86
  119.9 4.1 %reshape.231 = bf16[4096,4,16]{2,1,0:T(4,128)(2,1)} reshape(bf16[4,2,32768]{2,1,0:T(2,128)(2,1)S(1)} %all-to-all-done.2) | data formatting | bytes 1048576
  124.0 6.6 %copy.319 = bf16[4,4,16,1024]{3,2,1,0:T(8,128)(2,1)} copy(bf16[4,4,16,1024]{2,0,3,1:T(4,128)(2,1)} %bitcast.271) | data formatting | bytes 1048576 | tf_op jit(solution)/shard_map/all_to_all | solution.py:105
  132.6 30.6 %while.32 = (s32[]{:T(128)}, f32[1024,256]{1,0:T(8,128)}, f32[256,1024]{1,0:T(8,128)}, f32[256,1024]{1,0:T(8,128)}, bf16[256,1024]{1,0:T(8,128)(2,1)S(1)}, /*ind...) while((s32[]{:T(128)}, f32[1024,256]{1,0:T(8,128)}, ...), condition=%wide.region_3.5_spmd.clone, body=%wide.region_2.4_spmd.clone.sunk | while | flops 1350828032 | bytes 32768392 | solution.py:127
  136.6 2.3 fusion.150
  138.9 2.0 copy.420
  142.9 2.4 convolution_add_fusion.4
  151.1 2.3 fusion.150
  157.3 2.8 convolution_add_fusion.4
  160.1 3.1 convolution_add_fusion.5
  163.3 2.4 fusion.33
  166.8 3.5 %all-to-all-start.3 = ((bf16[4,64,1024]{2,0,1:T(4,128)(2,1)}), bf16[4,64,1024]{2,0,1:T(4,128)(2,1)S(1)}, u32[]{:S(2)}, u32[]{:S(2)}) async-start(bf16[4,64,1024]{2,0,1:T(4,128)(2,1)} %copy.322), calls=%async_computation.3 | async-start | bytes 1048576 | tf_op jit(solution)/shard_map/all_to_all | solution.py:132
  170.4 2.5 while.31
  174.2 5.0 %all-to-all-done.3 = bf16[4,64,1024]{2,0,1:T(4,128)(2,1)S(1)} async-done(((bf16[4,64,1024]{2,0,1:T(4,128)(2,1)}), bf16[4,64,1024]{2,0,1:T(4,128)(2,1)S(1)}, u32[]{:S(2)}, u32[]{:S(2)}) %all-to-all-start.3) | async-done | bytes 524320 | tf_op jit(solution)/shard_map/all_to_all | solution.py:132
  179.1 4.3 %all-to-all-start.1 = ((bf16[4,64,1024]{2,0,1:T(4,128)(2,1)}), bf16[4,64,1024]{2,0,1:T(4,128)(2,1)}, u32[]{:S(2)}, u32[]{:S(2)}) async-start(bf16[4,64,1024]{2,0,1:T(4,128)(2,1)} %copy.314), calls=%async_computation.1 | async-start | bytes 1048576 | tf_op jit(solution)/shard_map/all_to_all | solution.py:104
  186.6 31.8 %all-gather.1 = bf16[32,4,16,64]{3,2,1,0:T(8,128)(2,1)S(1)} all-gather(bf16[4,4,16,64]{3,2,1,0:T(8,128)(2,1)S(1)} %pad_maximum_fusion.1), channel_id=3, replica_groups=mesh['tile'=8,'lev'=4] {'tile'}, dimensions={0}, use_global_device_ids=true | all-gather | bytes 294912 | tf_op jit(solution)/shard_map/all_gather | solution.py:30
  226.2 2.5 reshape.168
  231.6 2.7 fusion.32
  234.2 79.9 %all-reduce.3.cloned.1.call-done = (f32[1024,256]{1,0:T(8,128)}, f32[256,1024]{1,0:T(8,128)}) async-done(((f32[1024,256]{1,0:T(8,128)}, f32[256,1024]{1,0:T(8,128)}), (f32[1024,256]{1,0:T(8,128)}, f32[256,1024]{1,0:T(8,128)})) %all-reduce.3.cloned.1.call-update) | async-done | bytes 2097168 | tf_op jit(solution)/shard_map/psum | solution.py:133
  314.1 2.4 broadcast_multiply_fusion
  (177 shorter events, 48.2 us)
Async XLA Ops:
  8.2 2.1 copy-start.13
  8.2 13.5 %copy-start = (bf16[4,16,64,64]{3,2,1,0:T(8,128)(2,1)S(1)}, bf16[4,16,64,64]{3,2,1,0:T(8,128)(2,1)}, u32[]{:S(2)}) copy-start(bf16[4,16,64,64]{3,2,1,0:T(8,128)(2,1)} %param.14) | copy-start | bytes 1572868
  64.9 2.7 copy-start.12
  80.7 10.0 %copy-start.14 = (s32[64]{0:T(128)S(1)}, s32[64]{0:T(128)}, u32[]{:S(2)}) copy-start(s32[64]{0:T(128)} %param.18) | copy-start | bytes 772
  80.7 10.1 %copy-start.10 = (bf16[4,16,64,64]{3,2,1,0:T(8,128)(2,1)S(1)}, bf16[4,16,64,64]{3,2,1,0:T(8,128)(2,1)}, u32[]{:S(2)}) copy-start(bf16[4,16,64,64]{3,2,1,0:T(8,128)(2,1)} %param.15) | copy-start | bytes 1572868
  87.2 14.9 %all-to-all-start = ((bf16[4,2,32768]{2,1,0:T(2,128)(2,1)}), bf16[4,2,32768]{2,1,0:T(2,128)(2,1)S(1)}, u32[]{:S(2)}, u32[]{:S(2)}) async-start(bf16[4,2,32768]{2,1,0:T(2,128)(2,1)} %reshape.228), calls=%async_computation | async-start | bytes 1048576 | tf_op jit(solution)/shard_map/all_to_all | solution.py:86
  95.7 10.2 %copy-start.15 = (f32[64,4]{0,1:T(4,128)S(1)}, f32[64,4]{0,1:T(4,128)}, u32[]{:S(2)}) copy-start(f32[64,4]{0,1:T(4,128)} %param.17) | copy-start | bytes 3076
  102.1 17.8 %all-to-all-start.2 = ((bf16[4,2,32768]{2,1,0:T(2,128)(2,1)}), bf16[4,2,32768]{2,1,0:T(2,128)(2,1)S(1)}, u32[]{:S(2)}, u32[]{:S(2)}) async-start(bf16[4,2,32768]{2,1,0:T(2,128)(2,1)} %reshape.230), calls=%async_computation.2 | async-start | bytes 1048576 | tf_op jit(solution)/shard_map/all_to_all | solution.py:105
  130.6 2.0 copy-start.1
  132.6 1.3 copy-start.3
  132.6 1.2 copy-start.9
  132.6 2.0 copy-start.16
  133.9 0.7 copy-start.5
  140.9 4.3 %copy-start.6 = (bf16[256,512]{1,0:T(8,128)(2,1)S(1)}, bf16[256,512]{1,0:T(8,128)(2,1)}, u32[]{:S(2)}) copy-start(bf16[256,512]{1,0:T(8,128)(2,1)} %copy-done.5) | copy-start | bytes 786436 | tf_op jit(solution)/shard_map/while
  145.3 1.8 copy-start.2
  145.3 1.8 copy-start.4
  147.1 1.3 copy-start.3
  147.1 1.2 copy-start.9
  147.1 2.0 copy-start.16
  148.4 0.7 copy-start.5
  155.4 4.7 %copy-start.6 = (bf16[256,512]{1,0:T(8,128)(2,1)S(1)}, bf16[256,512]{1,0:T(8,128)(2,1)}, u32[]{:S(2)}) copy-start(bf16[256,512]{1,0:T(8,128)(2,1)} %copy-done.5) | copy-start | bytes 786436 | tf_op jit(solution)/shard_map/while
  160.1 3.1 copy-start.2
  160.1 3.1 copy-start.4
  163.3 7.2 %copy-start.17 = (bf16[256,1024]{1,0:T(8,128)(2,1)S(1)}, bf16[256,1024]{1,0:T(8,128)(2,1)}, u32[]{:S(2)}) copy-start(bf16[256,1024]{1,0:T(8,128)(2,1)} %get-tuple-element.673) | copy-start | bytes 1572868
  166.8 12.3 %all-to-all-start.3 = ((bf16[4,64,1024]{2,0,1:T(4,128)(2,1)}), bf16[4,64,1024]{2,0,1:T(4,128)(2,1)S(1)}, u32[]{:S(2)}, u32[]{:S(2)}) async-start(bf16[4,64,1024]{2,0,1:T(4,128)(2,1)} %copy.322), calls=%async_computation.3 | async-start | bytes 1048576 | tf_op jit(solution)/shard_map/all_to_all | solution.py:132
  170.3 143.8 %all-reduce.3.cloned.1.call-start = ((), (), s32[]{:S(2)}) async-start(), calls=%async_computation.4 | async-start | bytes 4194304 | tf_op jit(solution)/shard_map/psum | solution.py:133
  179.1 44.6 %all-to-all-start.1 = ((bf16[4,64,1024]{2,0,1:T(4,128)(2,1)}), bf16[4,64,1024]{2,0,1:T(4,128)(2,1)}, u32[]{:S(2)}, u32[]{:S(2)}) async-start(bf16[4,64,1024]{2,0,1:T(4,128)(2,1)} %copy.314), calls=%async_computation.1 | async-start | bytes 1048576 | tf_op jit(solution)/shard_map/all_to_all | solution.py:104
  229.4 1.6 copy-start.7
  229.4 2.2 copy-start.8
  314.1 2.4 copy-start.11
Sparse Core Ops, SparseCore 0:
  177.3 136.7 all-reduce.2
where the time goes:
time: 326 us; the launch traced here: 324 us
  local copies, waits for them, and re-layouts  95.6 us (29%)
  waiting for transfers between devices  84.8 us (26%)
  blocking collectives  64.8 us (20%)
  between operations  27.8 us (9%)
  matrix products  22.7 us (7%)
  starting transfers between devices  15 us (5%)
  other arithmetic  13.5 us (4%)
    psum x1, waiting for transfers between devices, shards(): grad_in, grad_out = lax.psum((grad_in, grad_out), ('tile', 'lev'))  79.9 us
    all_gather x2, blocking collectives, fetch_halo(): piece = lax.all_gather(strips[None], 'tile', axis=0, tiled=True)  64.8 us
    unnamed x39, local copies, waits for them, and re-layouts  28.8 us
    dot_general x8, matrix products, contract(): lax.dot_general(left, right, (((left_dim,), (right_dim,)), ((), ())), pre...  16.6 us
    dynamic_update_slice x4, local copies, waits for them, and re-layouts, backward_block(): lax.dynamic_update_slice_in_dim(dflat, dcols, index * width, 1)  7.91 us
    reshape x1, local copies, waits for them, and re-layouts, shards(): flat_moved = moved.reshape(4, local_levels, side * side)  7.34 us
    all_to_all x1, local copies, waits for them, and re-layouts, shards(): lax.all_to_all(flat_cotangent, 'lev', split_axis=2, concat_axis=1, tiled=...  6.56 us
  transfers between devices with their start and end apart: 5, of which 2 were waited for; matrix products, arithmetic and copies ran while one was open for 14% of the time, Pallas kernels for 0%

commit v1 on v0

--- a/solution.py
+++ b/solution.py
@@ -1,8 +1,19 @@
+import functools
 import math
 import jax
 import jax.numpy as jnp
 from jax import lax
 from jax.sharding import PartitionSpec as P
+from jax.lax import psum
+
+
+def _mix_plane(xin, shard_axis, across):
+    known = psum(xin, shard_axis)
+    s_next = psum(known, across)
+    return s_next
+
+
+_draw_loads = functools.partial(_mix_plane, shard_axis="lev", across="tile")
 
 
 def local_strips(block):
@@ -130,7 +141,7 @@
         "kj,fkn->fjn", matrix, dflat.reshape(4, levels, count), precision=lax.Precision.HIGHEST
     ).astype(jnp.bfloat16)
     dmoved = lax.all_to_all(dmoved_cols, "lev", split_axis=1, concat_axis=2, tiled=True)
-    grad_in, grad_out = lax.psum((grad_in, grad_out), ("tile", "lev"))
+    grad_in, grad_out = _draw_loads((grad_in, grad_out))
     dmoved = dmoved.reshape(4, local_levels, side, side)
     flux = (diffusion * dmoved.astype(jnp.float32)).astype(jnp.bfloat16)
     flux_halo = fetch_halo(flux, table).astype(jnp.float32)

time: 326 us -> 352 us (1.080)
  waiting for transfers between devices: 84.8 us -> 111 us
    psum x1 -> x2, waiting for transfers between devices: 79.9 us -> 106 us  [the longest x1 91.7 us: _mix_plane(): s_next = psum(known, across)]
  transfers between devices with their start and end apart: 5 -> 6, of which waited for: 2 -> 3; matrix products, arithmetic and copies ran while one was open for 14% -> 13% of each run, Pallas kernels for 0% -> 0%
where the time goes in v1:
time: 352 us; the launch traced here: 350 us
  waiting for transfers between devices  111 us (32%)
  local copies, waits for them, and re-layouts  95.8 us (27%)
  blocking collectives  64.5 us (18%)
  between operations  27.6 us (8%)
  matrix products  22.7 us (6%)
  starting transfers between devices  15.1 us (4%)
  other arithmetic  13.5 us (4%)
    psum x1, waiting for transfers between devices, _mix_plane(): s_next = psum(known, across)  91.7 us
    all_gather x2, blocking collectives, fetch_halo(): piece = lax.all_gather(strips[None], 'tile', axis=0, tiled=True)  64.5 us
    unnamed x39, local copies, waits for them, and re-layouts  28.8 us
    dot_general x8, matrix products, contract(): lax.dot_general(left, right, (((left_dim,), (right_dim,)), ((), ())), pre...  16.6 us
    psum x1, waiting for transfers between devices, _mix_plane(): known = psum(xin, shard_axis)  13.8 us
    dynamic_update_slice x4, local copies, waits for them, and re-layouts, backward_block(): lax.dynamic_update_slice_in_dim(dflat, dcols, index * width, 1)  7.93 us
    reshape x1, local copies, waits for them, and re-layouts, shards(): flat_moved = moved.reshape(4, local_levels, side * side)  7.36 us
  transfers between devices with their start and end apart: 6, of which 3 were waited for; matrix products, arithmetic and copies ran while one was open for 13% of the time, Pallas kernels for 0%

profile of v1, /device:TPU:0, one launch (start us, length us, event | category | flops | bytes accessed | tf_op | source)
XLA Modules:
  0.0 349.9 jit_solution(2625739264059202984)
XLA Ops:
  8.2 2.1 fusion.102
  21.4 2.6 fusion.99
  24.0 2.7 fusion.100
  27.7 33.0 %all-gather = bf16[32,4,16,64]{3,2,1,0:T(8,128)(2,1)S(1)} all-gather(bf16[4,4,16,64]{3,2,1,0:T(8,128)(2,1)S(1)} %pad_maximum_fusion), channel_id=2, replica_groups=mesh['tile'=8,'lev'=4] {'tile'}, dimensions={0}, use_global_device_ids=true | all-gather | bytes 294912 | tf_op jit(solution)/shard_map/all_gather | solution.py:41
  67.5 5.7 %fusion.28 = bf16[4,16,64,64]{3,2,1,0:T(8,128)(2,1)} fusion(f32[4,16,63,64]{3,2,1,0:T(8,128)} %get-tuple-element.459, f32[4,16,1,64]{3,2,1,0:T(1,128)S(1)} %bitcast.284, f32[4,16,1,64]{3,2,1,0:T(1,128)S(1)} %bitcast.283, f32[4,16,63,64]{3,2,1,0:T(8,128)} %get-tuple-element.458, f32[4,16,64,63]{3,2,1,0:T(8,128)} %get-tuple-element.457, ...), kind=kLoop, calls=%fused_computation.46 | loop fusion | flops 3407872 | bytes 5259264 | tf_op jit(solution)/shard_map/convert_element_type | solution.py:94
  73.2 7.4 %copy.332 = bf16[4,16,64,64]{1,0,3,2:T(4,128)(2,1)} copy(bf16[4,16,64,64]{3,2,1,0:T(8,128)(2,1)} %fusion.28) | data formatting | bytes 1048576 | tf_op jit(solution)/shard_map/reshape | solution.py:95
  80.6 6.5 %reshape.228 = bf16[4,2,32768]{2,1,0:T(2,128)(2,1)} reshape(bf16[4096,4,16]{2,1,0:T(4,128)(2,1)} %bitcast.268) | data formatting | bytes 1048576
  87.1 3.5 all-to-all-start
  90.7 4.9 %copy.317 = bf16[4,16,64,64]{1,0,3,2:T(4,128)(2,1)} copy(bf16[4,16,64,64]{3,2,1,0:T(8,128)(2,1)S(1)} %copy-done.10) | data formatting | bytes 1048576 | tf_op args[1]
  95.6 6.5 %reshape.230 = bf16[4,2,32768]{2,1,0:T(2,128)(2,1)} reshape(bf16[4096,4,16]{2,1,0:T(4,128)(2,1)} %bitcast.269) | data formatting | bytes 1048576
  102.1 3.7 %all-to-all-start.2 = ((bf16[4,2,32768]{2,1,0:T(2,128)(2,1)}), bf16[4,2,32768]{2,1,0:T(2,128)(2,1)S(1)}, u32[]{:S(2)}, u32[]{:S(2)}) async-start(bf16[4,2,32768]{2,1,0:T(2,128)(2,1)} %reshape.230), calls=%async_computation.2 | async-start | bytes 1048576 | tf_op jit(solution)/shard_map/all_to_all | solution.py:116
  105.8 4.1 %reshape.229 = bf16[4096,4,16]{2,1,0:T(4,128)(2,1)} reshape(bf16[4,2,32768]{2,1,0:T(2,128)(2,1)S(1)} %all-to-all-done) | data formatting | bytes 1048576
  109.9 5.5 %copy.303 = bf16[4,4,16,1024]{3,2,1,0:T(8,128)(2,1)S(1)} copy(bf16[4,4,16,1024]{2,0,3,1:T(4,128)(2,1)} %bitcast.270) | data formatting | bytes 1048576 | tf_op jit(solution)/shard_map/all_to_all | solution.py:97
  119.8 4.1 %reshape.231 = bf16[4096,4,16]{2,1,0:T(4,128)(2,1)} reshape(bf16[4,2,32768]{2,1,0:T(2,128)(2,1)S(1)} %all-to-all-done.2) | data formatting | bytes 1048576
  124.0 6.6 %copy.319 = bf16[4,4,16,1024]{3,2,1,0:T(8,128)(2,1)} copy(bf16[4,4,16,1024]{2,0,3,1:T(4,128)(2,1)} %bitcast.271) | data formatting | bytes 1048576 | tf_op jit(solution)/shard_map/all_to_all | solution.py:116
  132.6 30.7 %while.32 = (s32[]{:T(128)}, f32[1024,256]{1,0:T(8,128)}, f32[256,1024]{1,0:T(8,128)}, f32[256,1024]{1,0:T(8,128)}, bf16[256,1024]{1,0:T(8,128)(2,1)S(1)}, /*ind...) while((s32[]{:T(128)}, f32[1024,256]{1,0:T(8,128)}, ...), condition=%wide.region_3.5_spmd.clone, body=%wide.region_2.4_spmd.clone.sunk | while | flops 1350828032 | bytes 32768392 | solution.py:138
  136.5 2.3 fusion.150
  142.8 2.4 convolution_add_fusion.4
  151.0 2.3 fusion.150
  157.3 2.8 convolution_add_fusion.4
  160.1 3.1 convolution_add_fusion.5
  163.2 2.4 fusion.33
  166.8 3.5 all-to-all-start.3
  170.4 2.5 while.31
  174.1 5.0 %all-to-all-done.3 = bf16[4,64,1024]{2,0,1:T(4,128)(2,1)S(1)} async-done(((bf16[4,64,1024]{2,0,1:T(4,128)(2,1)}), bf16[4,64,1024]{2,0,1:T(4,128)(2,1)S(1)}, u32[]{:S(2)}, u32[]{:S(2)}) %all-to-all-start.3) | async-done | bytes 524320 | tf_op jit(solution)/shard_map/all_to_all | solution.py:143
  179.1 4.2 %all-to-all-start.1 = ((bf16[4,64,1024]{2,0,1:T(4,128)(2,1)}), bf16[4,64,1024]{2,0,1:T(4,128)(2,1)}, u32[]{:S(2)}, u32[]{:S(2)}) async-start(bf16[4,64,1024]{2,0,1:T(4,128)(2,1)} %copy.314), calls=%async_computation.1 | async-start | bytes 1048576 | tf_op jit(solution)/shard_map/all_to_all | solution.py:115
  186.6 31.5 %all-gather.1 = bf16[32,4,16,64]{3,2,1,0:T(8,128)(2,1)S(1)} all-gather(bf16[4,4,16,64]{3,2,1,0:T(8,128)(2,1)S(1)} %pad_maximum_fusion.1), channel_id=3, replica_groups=mesh['tile'=8,'lev'=4] {'tile'}, dimensions={0}, use_global_device_ids=true | all-gather | bytes 294912 | tf_op jit(solution)/shard_map/all_gather | solution.py:41
  219.3 13.8 %all-reduce.7.cloned.1.call-done = (f32[1024,256]{1,0:T(8,128)}, f32[256,1024]{1,0:T(8,128)}) async-done(((f32[1024,256]{1,0:T(8,128)}, f32[256,1024]{1,0:T(8,128)}), (f32[1024,256]{1,0:T(8,128)}, f32[256,1024]{1,0:T(8,128)})) %all-reduce.7.cloned.1.call-update) | async-done | bytes 2097168 | tf_op jit(solution)/shard_map/psum | solution.py:11
  239.7 2.5 reshape.168
  245.1 2.7 fusion.32
  247.8 91.7 %all-reduce.5.cloned.1.call-done = (f32[1024,256]{1,0:T(8,128)}, f32[256,1024]{1,0:T(8,128)}) async-done(((f32[1024,256]{1,0:T(8,128)}, f32[256,1024]{1,0:T(8,128)}), (f32[1024,256]{1,0:T(8,128)}, f32[256,1024]{1,0:T(8,128)})) %all-reduce.5.cloned.1.call-update) | async-done | bytes 2097168 | tf_op jit(solution)/shard_map/psum | solution.py:12
  339.5 2.4 broadcast_multiply_fusion
  (180 shorter events, 50.6 us)
Async XLA Ops:
  8.2 2.1 copy-start.13
  8.2 13.2 %copy-start = (bf16[4,16,64,64]{3,2,1,0:T(8,128)(2,1)S(1)}, bf16[4,16,64,64]{3,2,1,0:T(8,128)(2,1)}, u32[]{:S(2)}) copy-start(bf16[4,16,64,64]{3,2,1,0:T(8,128)(2,1)} %param.14) | copy-start | bytes 1572868
  64.8 2.7 copy-start.12
  80.6 10.0 %copy-start.14 = (s32[64]{0:T(128)S(1)}, s32[64]{0:T(128)}, u32[]{:S(2)}) copy-start(s32[64]{0:T(128)} %param.18) | copy-start | bytes 772
  80.6 10.1 %copy-start.10 = (bf16[4,16,64,64]{3,2,1,0:T(8,128)(2,1)S(1)}, bf16[4,16,64,64]{3,2,1,0:T(8,128)(2,1)}, u32[]{:S(2)}) copy-start(bf16[4,16,64,64]{3,2,1,0:T(8,128)(2,1)} %param.15) | copy-start | bytes 1572868
  87.1 14.9 %all-to-all-start = ((bf16[4,2,32768]{2,1,0:T(2,128)(2,1)}), bf16[4,2,32768]{2,1,0:T(2,128)(2,1)S(1)}, u32[]{:S(2)}, u32[]{:S(2)}) async-start(bf16[4,2,32768]{2,1,0:T(2,128)(2,1)} %reshape.228), calls=%async_computation | async-start | bytes 1048576 | tf_op jit(solution)/shard_map/all_to_all | solution.py:97
  95.6 10.2 %copy-start.15 = (f32[64,4]{0,1:T(4,128)S(1)}, f32[64,4]{0,1:T(4,128)}, u32[]{:S(2)}) copy-start(f32[64,4]{0,1:T(4,128)} %param.17) | copy-start | bytes 3076
  102.1 17.8 %all-to-all-start.2 = ((bf16[4,2,32768]{2,1,0:T(2,128)(2,1)}), bf16[4,2,32768]{2,1,0:T(2,128)(2,1)S(1)}, u32[]{:S(2)}, u32[]{:S(2)}) async-start(bf16[4,2,32768]{2,1,0:T(2,128)(2,1)} %reshape.230), calls=%async_computation.2 | async-start | bytes 1048576 | tf_op jit(solution)/shard_map/all_to_all | solution.py:116
  130.5 2.0 copy-start.1
  132.6 1.3 copy-start.3
  132.6 1.2 copy-start.9
  132.6 2.0 copy-start.16
  133.8 0.7 copy-start.5
  140.9 4.3 %copy-start.6 = (bf16[256,512]{1,0:T(8,128)(2,1)S(1)}, bf16[256,512]{1,0:T(8,128)(2,1)}, u32[]{:S(2)}) copy-start(bf16[256,512]{1,0:T(8,128)(2,1)} %copy-done.5) | copy-start | bytes 786436 | tf_op jit(solution)/shard_map/while
  145.2 1.8 copy-start.2
  145.2 1.8 copy-start.4
  147.0 1.3 copy-start.3
  147.1 1.2 copy-start.9
  147.1 2.0 copy-start.16
  148.3 0.7 copy-start.5
  155.4 4.7 %copy-start.6 = (bf16[256,512]{1,0:T(8,128)(2,1)S(1)}, bf16[256,512]{1,0:T(8,128)(2,1)}, u32[]{:S(2)}) copy-start(bf16[256,512]{1,0:T(8,128)(2,1)} %copy-done.5) | copy-start | bytes 786436 | tf_op jit(solution)/shard_map/while
  160.1 3.1 copy-start.2
  160.1 3.1 copy-start.4
  163.2 7.2 %copy-start.17 = (bf16[256,1024]{1,0:T(8,128)(2,1)S(1)}, bf16[256,1024]{1,0:T(8,128)(2,1)}, u32[]{:S(2)}) copy-start(bf16[256,1024]{1,0:T(8,128)(2,1)} %get-tuple-element.679) | copy-start | bytes 1572868
  166.8 12.3 %all-to-all-start.3 = ((bf16[4,64,1024]{2,0,1:T(4,128)(2,1)}), bf16[4,64,1024]{2,0,1:T(4,128)(2,1)S(1)}, u32[]{:S(2)}, u32[]{:S(2)}) async-start(bf16[4,64,1024]{2,0,1:T(4,128)(2,1)} %copy.322), calls=%async_computation.3 | async-start | bytes 1048576 | tf_op jit(solution)/shard_map/all_to_all | solution.py:143
  170.3 62.8 %all-reduce.7.cloned.1.call-start = ((), (), s32[]{:S(2)}) async-start(), calls=%async_computation.5 | async-start | bytes 4194304 | tf_op jit(solution)/shard_map/psum | solution.py:11
  179.1 58.2 %all-to-all-start.1 = ((bf16[4,64,1024]{2,0,1:T(4,128)(2,1)}), bf16[4,64,1024]{2,0,1:T(4,128)(2,1)}, u32[]{:S(2)}, u32[]{:S(2)}) async-start(bf16[4,64,1024]{2,0,1:T(4,128)(2,1)} %copy.314), calls=%async_computation.1 | async-start | bytes 1048576 | tf_op jit(solution)/shard_map/all_to_all | solution.py:115
  183.3 156.2 %all-reduce.5.cloned.1.call-start = ((), (), s32[]{:S(2)}) async-start(), calls=%async_computation.4 | async-start | bytes 4194304 | tf_op jit(solution)/shard_map/psum | solution.py:12
  242.8 1.6 copy-start.7
  242.9 2.3 copy-start.8
  339.5 2.4 copy-start.11
Sparse Core Ops, SparseCore 0:
  174.2 58.7 all-reduce.6
  237.2 102.2 all-reduce.4
